TPU v7x, 32 devices: a whole 2x2x4 slice. The times are simulated.
32 devices in a mesh: grp: 2 (over x), row: 16 (over z, y, core).
Axes of the slice: x: 2, y: 2, z: 4, core: 2. Of those that a mesh axis runs over, the one named last changes fastest.
Arguments:
- matrix: bfloat16 [32, 2048, 16384], P(('grp', 'row')), parts along dimension 0, may hold values from -1 to 1
- probes: bfloat16 [16384, 128], P(('grp', 'row')), parts along dimension 0, may hold values from -6 to 6
Outputs:
- basis_out: bfloat16 [16384, 128], P(('grp', 'row')), parts along dimension 0
- sketch_out: bfloat16 [32, 4096, 128], P(('grp', 'row')), parts along dimension 0
There are 2 independent parts, one for each index of `grp`. A program takes and returns all parts, laid end to end along the dimension named above; each array names one. Nothing has to cross between parts.
All inputs are finite; a program needn't handle non-finite values.
Results may differ from a plain program's by a relative error of at most 0.012.
Values may be sent and summed in bfloat16 or wider, within the bound.
A program may use at most 192 MiB of HBM per device.

v0:
```python
import math

import jax
import jax.numpy as jnp
from jax import lax
from jax.sharding import PartitionSpec as P

GRID_ROWS = 4
ITERS = 2


def from_partner(shard, axis, bit):
    return lax.ppermute(shard, axis, [(i, i ^ 1 << bit) for i in range(lax.axis_size(axis))])


def orthonormal(product, gram_matrix, rescale):
    factor = jnp.linalg.cholesky(gram_matrix)
    solved = lax.linalg.triangular_solve(
        factor, product, left_side=False, lower=True, transpose_a=True
    )
    return (solved * rescale).astype(jnp.bfloat16)


def digit_set(device, level):
    return device // 2**level % 2 == 1


def per_device(matrix, probes):
    tile_block = matrix[0]
    tile_rows = tile_block.shape[0]
    grid_cols = lax.axis_size("row") // GRID_ROWS
    col_levels = grid_cols.bit_length() - 1
    row_levels = GRID_ROWS.bit_length() - 1
    device = lax.axis_index("row")
    rescale = math.sqrt(GRID_ROWS * tile_rows)
    current = probes
    sketch_block = None
    for iteration in range(ITERS):
        panel = current
        for level in range(col_levels):
            other = from_partner(panel, "row", level)
            panel = jnp.where(
                digit_set(device, level),
                jnp.concatenate([other, panel], 0),
                jnp.concatenate([panel, other], 0),
            )
        partial_value = lax.dot_general(
            tile_block, panel, (((0,), (0,)), ((), ())), preferred_element_type=jnp.float32
        )
        for level in range(row_levels):
            partial_value = partial_value + from_partner(
                partial_value.astype(jnp.bfloat16), "row", col_levels + level
            ).astype(partial_value.dtype)
        sketch = partial_value.astype(jnp.bfloat16)
        share_rows = sketch.shape[0] // GRID_ROWS
        grid_row = device // grid_cols
        sketch_block = lax.dynamic_slice_in_dim(sketch, grid_row * share_rows, share_rows, 0)
        image = jnp.dot(tile_block, sketch, preferred_element_type=jnp.float32)
        for level in reversed(range(col_levels)):
            half_rows = image.shape[0] // 2
            lower_part = image[:half_rows]
            upper_part = image[half_rows:]
            upward = digit_set(device, level)
            sent = jnp.where(upward, lower_part, upper_part)
            kept = jnp.where(upward, upper_part, lower_part)
            image = kept + from_partner(sent.astype(jnp.bfloat16), "row", level).astype(sent.dtype)
        local_gram = jnp.dot(
            image.T, image, precision=lax.Precision.HIGHEST, preferred_element_type=jnp.float32
        )
        gram_matrix = lax.psum(local_gram, "row")
        current = orthonormal(image, gram_matrix, rescale)
    return (current, sketch_block[None])


def solution(mesh):
    placed = (P(("grp", "row"), None, None), P(("grp", "row"), None))
    return jax.shard_map(
        per_device,
        mesh=mesh,
        in_specs=placed,
        out_specs=(P(("grp", "row"), None), P(("grp", "row"), None, None)),
        check_vma=False,
    )
```

profile of v0, /device:TPU:8, one launch (start us, length us, event | category | flops | bytes accessed | tf_op | source)
XLA Modules:
  0.0 968.9 jit_solution(17788045940890955766)
XLA Ops:
  8.3 1.3 collective-permute-done
  9.7 1.6 collective-permute-start.1
  11.3 6.8 collective-permute-done.1
  18.2 28.6 %fusion.50 = (bf16[16384,128]{0,1:T(8,128)(2,1)}, f32[16384,128]{0,1:T(8,128)}) fusion(bf16[1,2048,16384]{2,1,0:T(8,128)(2,1)} %param.5, bf16[1024,128]{0,1:T(8,128)(2,1)S(1)} %maximum_select_fusion.4, bf16[1024,128]{0,1:T(8,128)(2,1)S(1)} %collective-permute-done.1, pred[]{:T(512)S(6)} %eq.22), kind=kOutput, calls=%fused_computation.70 | convolution fusion | flops 8594391040 | bytes 80216064 | tf_op jit(solution)/shard_map/dot_general | solution.py:47
  47.0 91.8 %collective-permute-done.2 = bf16[16384,128]{0,1:T(8,128)(2,1)S(1)} collective-permute-done((bf16[16384,128]{0,1:T(8,128)(2,1)}, bf16[16384,128]{0,1:T(8,128)(2,1)S(1)}, u32[]{:S(2)}, u32[]{:S(2)}) %collective-permute-start.2) | collective-permute-done | bytes 4194336 | tf_op jit(solution)/shard_map/ppermute | solution.py:13
  138.8 5.7 fusion.14
  144.5 2.7 collective-permute-start.3
  147.1 178.2 %collective-permute-done.3 = bf16[16384,128]{0,1:T(8,128)(2,1)} collective-permute-done((bf16[16384,128]{0,1:T(8,128)(2,1)S(1)}, bf16[16384,128]{0,1:T(8,128)(2,1)}, u32[]{:S(2)}, u32[]{:S(2)}) %collective-permute-start.3) | collective-permute-done | bytes 4194336 | tf_op jit(solution)/shard_map/ppermute | solution.py:13
  325.3 33.8 %fusion.16 = f32[2048,128]{0,1:T(8,128)S(1)} fusion(bf16[1,2048,16384]{2,1,0:T(8,128)(2,1)} %param.5, bf16[16384,128]{0,1:T(8,128)(2,1)} %collective-permute-done.3, f32[16384,128]{0,1:T(8,128)} %get-tuple-element.9, bf16[16384,128]{0,1:T(8,128)(2,1)} %copy-done), kind=kOutput, calls=%fused_computation.16 | convolution fusion | flops 8600420352 | bytes 84934656 | tf_op jit(solution)/shard_map/dot_general | solution.py:58
  359.2 1.6 collective-permute-start.4
  360.8 6.7 collective-permute-done.4
  367.7 1.3 collective-permute-done.5
  369.0 1.0 fusion.46
  370.3 89.0 %all-reduce.3.cloned.1.call-done = f32[128,128]{0,1:T(8,128)} async-done(((f32[128,128]{0,1:T(8,128)}), f32[128,128]{0,1:T(8,128)}) %all-reduce.3.cloned.1.call-update) | async-done | bytes 65552 | tf_op jit(solution)/shard_map/psum | solution.py:70
  461.1 11.7 %cholesky.44 = f32[128,128]{1,0:T(8,128)S(1)} custom-call(f32[128,128]{1,0:T(8,128)S(1)} %fusion.43), custom_call_target="Cholesky" | custom-call | tf_op jit(solution)/shard_map/jit(cholesky)/cholesky | solution.py:17
  474.2 9.8 %custom-call.6 = f32[1,128,128]{1,2,0:T(8,128)S(1)} custom-call(f32[1,128,128]{2,1,0:T(8,128)S(1)} %fusion.38), custom_call_target="InvertDiagBlocksLowerTriangular" | custom-call | tf_op jit(solution)/shard_map/triangular_solve/custom-call.0 | solution.py:18
  484.5 1.3 collective-permute-done.6
  486.6 7.8 collective-permute-done.7
  494.4 28.6 %fusion.51 = (bf16[16384,128]{0,1:T(8,128)(2,1)}, f32[16384,128]{0,1:T(8,128)}) fusion(bf16[1,2048,16384]{2,1,0:T(8,128)(2,1)} %param.5, bf16[1024,128]{0,1:T(8,128)(2,1)S(1)} %maximum_select_fusion.5, bf16[1024,128]{0,1:T(8,128)(2,1)S(1)} %collective-permute-done.7, pred[]{:T(512)S(6)} %eq.22), kind=kOutput, calls=%fused_computation.71 | convolution fusion | flops 8594391040 | bytes 80216064 | tf_op jit(solution)/shard_map/dot_general | solution.py:47
  523.0 92.0 %collective-permute-done.8 = bf16[16384,128]{0,1:T(8,128)(2,1)S(1)} collective-permute-done((bf16[16384,128]{0,1:T(8,128)(2,1)}, bf16[16384,128]{0,1:T(8,128)(2,1)S(1)}, u32[]{:S(2)}, u32[]{:S(2)}) %collective-permute-start.8) | collective-permute-done | bytes 4194336 | tf_op jit(solution)/shard_map/ppermute | solution.py:13
  615.0 4.4 fusion.15
  619.4 1.5 collective-permute-start.9
  620.9 178.3 %collective-permute-done.9 = bf16[16384,128]{0,1:T(8,128)(2,1)} collective-permute-done((bf16[16384,128]{0,1:T(8,128)(2,1)S(1)}, bf16[16384,128]{0,1:T(8,128)(2,1)}, u32[]{:S(2)}, u32[]{:S(2)}) %collective-permute-start.9) | collective-permute-done | bytes 4194336 | tf_op jit(solution)/shard_map/ppermute | solution.py:13
  799.2 8.2 add_convert_fusion
  807.4 29.7 %fusion.19 = f32[2048,128]{0,1:T(8,128)S(1)} fusion(bf16[16384,128]{0,1:T(8,128)(2,1)} %add_convert_fusion, bf16[1,2048,16384]{2,1,0:T(8,128)(2,1)} %param.5), kind=kOutput, calls=%fused_computation.17 | convolution fusion | flops 8589934592 | bytes 72351744 | tf_op jit(solution)/shard_map/dot_general | solution.py:58
  837.6 7.8 collective-permute-done.10
  845.6 1.3 collective-permute-done.11
  848.0 1.3 constant_dynamic-slice_fusion
  849.3 1.3 copy.19
  850.6 85.7 %all-reduce.5.cloned.1.call-done = f32[128,128]{0,1:T(8,128)} async-done(((f32[128,128]{0,1:T(8,128)}), f32[128,128]{0,1:T(8,128)}) %all-reduce.5.cloned.1.call-update) | async-done | bytes 65552 | tf_op jit(solution)/shard_map/psum | solution.py:70
  938.0 11.7 %cholesky.55 = f32[128,128]{1,0:T(8,128)S(1)} custom-call(f32[128,128]{1,0:T(8,128)S(1)} %fusion.41), custom_call_target="Cholesky" | custom-call | tf_op jit(solution)/shard_map/jit(cholesky)/cholesky | solution.py:17
  951.1 9.8 %custom-call.7 = f32[1,128,128]{1,2,0:T(8,128)S(1)} custom-call(f32[1,128,128]{2,1,0:T(8,128)S(1)} %fusion.39), custom_call_target="InvertDiagBlocksLowerTriangular" | custom-call | tf_op jit(solution)/shard_map/triangular_solve/custom-call.0 | solution.py:18
  (37 shorter events, 12.3 us)
Async XLA Ops:
  7.2 452.2 %all-reduce.3.cloned.1.call-start = ((), (), s32[]{:S(2)}) async-start(), calls=%async_computation | async-start | bytes 131072 | tf_op jit(solution)/shard_map/psum | solution.py:70
  8.2 1.4 collective-permute-start
  9.7 8.4 collective-permute-start.1
  46.7 92.0 %collective-permute-start.2 = (bf16[16384,128]{0,1:T(8,128)(2,1)}, bf16[16384,128]{0,1:T(8,128)(2,1)S(1)}, u32[]{:S(2)}, u32[]{:S(2)}) collective-permute-start(bf16[16384,128]{0,1:T(8,128)(2,1)} %get-tuple-element.8), channel_id=1, source_target_pairs={{0,4},{1,5},{2,6},{3,7},{4,0},{5,1},{6,2},{7,3},{8,12},{9,13},{10,... | collective-permute-start | bytes 12582920 | tf_op jit(solution)/shard_map/ppermute | solution.py:13
  138.8 5.7 copy-start
  144.5 180.8 %collective-permute-start.3 = (bf16[16384,128]{0,1:T(8,128)(2,1)S(1)}, bf16[16384,128]{0,1:T(8,128)(2,1)}, u32[]{:S(2)}, u32[]{:S(2)}) collective-permute-start(bf16[16384,128]{0,1:T(8,128)(2,1)S(1)} %fusion.14), channel_id=1, source_target_pairs={{0,8},{1,9},{2,10},{3,11},{4,12},{5,13},{6,14},{7,15},{8,0},{9,1},... | collective-permute-start | bytes 12582920 | tf_op jit(solution)/shard_map/ppermute | solution.py:13
  359.2 8.3 collective-permute-start.4
  367.6 1.4 collective-permute-start.5
  370.1 566.2 %all-reduce.5.cloned.1.call-start = ((), (), s32[]{:S(2)}) async-start(), calls=%async_computation.1 | async-start | bytes 131072 | tf_op jit(solution)/shard_map/psum | solution.py:70
  484.4 1.4 collective-permute-start.6
  485.9 8.4 collective-permute-start.7
  523.0 92.0 %collective-permute-start.8 = (bf16[16384,128]{0,1:T(8,128)(2,1)}, bf16[16384,128]{0,1:T(8,128)(2,1)S(1)}, u32[]{:S(2)}, u32[]{:S(2)}) collective-permute-start(bf16[16384,128]{0,1:T(8,128)(2,1)} %get-tuple-element.10), channel_id=1, source_target_pairs={{0,4},{1,5},{2,6},{3,7},{4,0},{5,1},{6,2},{7,3},{8,12},{9,13},{10,... | collective-permute-start | bytes 12582920 | tf_op jit(solution)/shard_map/ppermute | solution.py:13
  619.4 179.8 %collective-permute-start.9 = (bf16[16384,128]{0,1:T(8,128)(2,1)S(1)}, bf16[16384,128]{0,1:T(8,128)(2,1)}, u32[]{:S(2)}, u32[]{:S(2)}) collective-permute-start(bf16[16384,128]{0,1:T(8,128)(2,1)S(1)} %fusion.15), channel_id=1, source_target_pairs={{0,8},{1,9},{2,10},{3,11},{4,12},{5,13},{6,14},{7,15},{8,0},{9,1},... | collective-permute-start | bytes 12582920 | tf_op jit(solution)/shard_map/ppermute | solution.py:13
  837.1 8.3 collective-permute-start.10
  845.5 1.4 collective-permute-start.11
Sparse Core Ops, SparseCore 0:
  370.2 89.0 all-reduce.2
  848.1 88.1 all-reduce.4
where the time goes:
time: 970 us; the launch traced here: 969 us
  waiting for transfers between devices  749 us (77%)
  matrix products  124 us (13%)
  other arithmetic  66.2 us (7%)
  between operations  14.3 us (1%)
    ppermute x12, waiting for transfers between devices, from_partner(): lax.ppermute(shard, axis, [(i, i ^ 1 << bit) for i in range(lax.axis_size...  575 us
    psum x2, waiting for transfers between devices, per_device(): gram_matrix = lax.psum(local_gram, 'row')  175 us
    dot_general x2, matrix products, per_device(): image = jnp.dot(tile_block, sketch, preferred_element_type=jnp.float32)  63.5 us
    dot_general x2, matrix products, per_device(): lax.dot_general(tile_block, panel, (((0,), (0,)), ((), ())), preferred_el...  57.2 us
    another operation x6, other arithmetic, orthonormal(): factor = jnp.linalg.cholesky(gram_matrix)  24.8 us
    another operation x4, other arithmetic, orthonormal(): lax.linalg.triangular_solve(factor, product, left_side=False, lower=True,...  20.9 us
  transfers between devices with their start and end apart: 14, of which 14 were waited for; matrix products, arithmetic and copies ran while one was open for 0% of the time, Pallas kernels for 0%

commit v1 on v0

v1 whole, which is shorter than its diff:
```python
import functools
import math

import jax
import jax.numpy as jnp
from jax import lax
from jax.experimental import pallas as pl
from jax.experimental.pallas import tpu as pltpu
from jax.sharding import PartitionSpec as P

GRID_ROWS = 4
ITERS = 2
CHUNK = 512
LAG_MID, LAG_SUM, LAG_END = 2, 4, 6
AHEAD = 3
WINDOW = AHEAD + LAG_END
MESH = pl.DeviceIdType.MESH


def remote(src, dst, send_sem, recv_sem, target):
    return pltpu.make_async_remote_copy(
        src_ref=src, dst_ref=dst, send_sem=send_sem, recv_sem=recv_sem,
        device_id={"row": target}, device_id_type=MESH,
    )


def stage_kernel(
    cols, chunk, a_ref, cur_ref, image_ref, gram_ref, block_ref,
    a_buf, own, outgoing, landed, crossed, total, panel, panel_t, acc,
    share_out, share_in, gram_row, gram_col,
    a_sem, send_a, send_b, recv_a, recv_b,
    panel_send, panel_recv, share_send, share_recv,
    row_send, row_recv, col_send, col_recv,
):
    me = lax.axis_index("row")
    grid_row, col = me // cols, lax.rem(me, cols)
    base = grid_row * cols
    slab = cur_ref.shape[0]
    steps = a_ref.shape[1] // chunk
    is_end = (grid_row == 0) | (grid_row == GRID_ROWS - 1)
    is_mid = jnp.logical_not(is_end)
    neighbour = (grid_row ^ 1) * cols + col
    opposite = (GRID_ROWS - 1 - grid_row) * cols + col

    def row_peer(off):
        return lax.rem(col + off, cols)

    def col_peer(off):
        return lax.rem(grid_row + off, GRID_ROWS)

    def each(count, body):
        lax.fori_loop(1, count, lambda off, c: (body(off), c)[1], 0)

    def fetch(step):
        slot = lax.rem(step, WINDOW)
        return pltpu.make_async_copy(
            a_ref.at[:, pl.ds(pl.multiple_of(step * chunk, chunk), chunk)],
            a_buf.at[slot], a_sem.at[slot],
        )

    for step in range(min(AHEAD, steps)):
        fetch(step).start()

    barrier = pltpu.get_barrier_semaphore()

    def greet(target):
        pl.semaphore_signal(barrier, inc=1, device_id={"row": target}, device_id_type=MESH)

    each(cols, lambda off: greet(base + row_peer(off)))
    each(GRID_ROWS, lambda off: greet(col_peer(off) * cols + col))
    pl.semaphore_wait(barrier, cols - 1 + GRID_ROWS - 1)

    def slab_of(index):
        return pl.ds(pl.multiple_of(index * slab, slab), slab)

    def panel_copy(sender, target):
        return remote(
            cur_ref, panel.at[slab_of(sender)], panel_send.at[target], panel_recv.at[sender],
            base + target,
        )

    each(cols, lambda off: panel_copy(col, row_peer(off)).start())
    panel[slab_of(col), :] = cur_ref[...]
    acc[...] = jnp.zeros_like(acc)
    each(cols, lambda off: panel_copy(row_peer(off), row_peer(off)).wait_recv())
    panel_t[...] = panel[...].astype(jnp.float32).T.astype(jnp.bfloat16)

    def rows_of(step):
        return pl.ds(pl.multiple_of(step * chunk, chunk), chunk)

    def to_neighbour(source, sem, step):
        return remote(
            source.at[rows_of(step)], landed.at[rows_of(step)], sem.at[step], recv_a.at[step],
            neighbour,
        )

    def to_opposite(step):
        return remote(
            outgoing.at[rows_of(step)], crossed.at[rows_of(step)], send_a.at[step],
            recv_b.at[step], opposite,
        )

    def body(step, carry):
        @pl.when(step < steps)
        def _():
            fetch(step).wait()
            part = jnp.dot(
                panel_t[...], a_buf[lax.rem(step, WINDOW)], preferred_element_type=jnp.float32
            ).T

            @pl.when(is_end)
            def _():
                outgoing[rows_of(step), :] = part.astype(jnp.bfloat16)
                to_neighbour(outgoing, send_a, step).start()

            @pl.when(is_mid)
            def _():
                own[lax.rem(step, WINDOW)] = part

        mid = step - LAG_MID

        @pl.when(is_mid & (mid >= 0) & (mid < steps))
        def _():
            slot = lax.rem(mid, WINDOW)
            to_neighbour(total, send_b, mid).wait_recv()
            pair = own[slot] + landed[rows_of(mid), :].astype(jnp.float32)
            own[slot] = pair
            outgoing[rows_of(mid), :] = pair.astype(jnp.bfloat16)
            to_opposite(mid).start()

        last = step - jnp.where(is_end, LAG_END, LAG_SUM)

        @pl.when((last >= 0) & (last < steps))
        def _():
            slot = lax.rem(last, WINDOW)

            @pl.when(is_mid)
            def _():
                to_opposite(last).wait_recv()
                whole = own[slot] + crossed[rows_of(last), :].astype(jnp.float32)
                total[rows_of(last), :] = whole.astype(jnp.bfloat16)
                to_neighbour(total, send_b, last).start()

            @pl.when(is_end)
            def _():
                to_neighbour(outgoing, send_a, last).wait_recv()
                total[rows_of(last), :] = landed[rows_of(last), :]

            acc[...] += jnp.dot(
                a_buf[slot], total[rows_of(last), :], preferred_element_type=jnp.float32
            )

        @pl.when(step + AHEAD < steps)
        def _():
            fetch(step + AHEAD).start()

        return carry

    lax.fori_loop(0, steps + LAG_END, body, 0)

    def share_copy(sender, target):
        return remote(
            share_out.at[slab_of(target)], share_in.at[sender], share_send.at[target],
            share_recv.at[sender], base + target,
        )

    share_out[...] = acc[...].astype(jnp.bfloat16)
    each(cols, lambda off: share_copy(col, row_peer(off)).start())
    share = block_ref.shape[0]
    block_ref[...] = total[pl.ds(pl.multiple_of(grid_row * share, share), share), :]
    image_ref[...] = acc[slab_of(col), :]

    def add_share(off):
        sender = row_peer(off)
        share_copy(sender, sender).wait_recv()
        image_ref[...] += share_in[sender].astype(jnp.float32)

    each(cols, add_share)

    def row_copy(sender, target):
        return remote(
            gram_row.at[col], gram_row.at[sender], row_send.at[target], row_recv.at[sender],
            base + target,
        )

    def col_copy(sender, target):
        return remote(
            gram_col.at[grid_row], gram_col.at[sender], col_send.at[target], col_recv.at[sender],
            target * cols + col,
        )

    image = image_ref[...]
    gram_row[col] = jnp.dot(
        image.T, image, precision=lax.Precision.HIGHEST, preferred_element_type=jnp.float32
    )
    each(cols, lambda off: row_copy(col, row_peer(off)).start())
    each(cols, lambda off: row_copy(row_peer(off), row_peer(off)).wait_recv())
    row_sum = lax.fori_loop(
        1, cols, lambda i, value: value + gram_row[i], gram_row[0]
    )
    gram_col[grid_row] = row_sum
    each(GRID_ROWS, lambda off: col_copy(grid_row, col_peer(off)).start())
    each(GRID_ROWS, lambda off: col_copy(col_peer(off), col_peer(off)).wait_recv())
    gram_ref[...] = (gram_col[0] + gram_col[1]) + (gram_col[2] + gram_col[3])

    each(cols, lambda off: panel_copy(col, row_peer(off)).wait_send())
    each(cols, lambda off: share_copy(col, row_peer(off)).wait_send())
    each(cols, lambda off: row_copy(col, row_peer(off)).wait_send())
    each(GRID_ROWS, lambda off: col_copy(grid_row, col_peer(off)).wait_send())

    def drain(step, carry):
        to_opposite(step).wait_send()

        @pl.when(is_mid)
        def _():
            to_neighbour(total, send_b, step).wait_send()

        return carry

    lax.fori_loop(0, steps, drain, 0)


def stage(tile, current, cols):
    rows, words = tile.shape
    slab, probes = current.shape
    chunk = min(CHUNK, words)
    steps = words // chunk
    half, full = jnp.bfloat16, jnp.float32
    sems = [
        (WINDOW,), (steps,), (steps,), (steps,), (steps,),
        (cols,), (cols,), (cols,), (cols,), (cols,), (cols,), (GRID_ROWS,), (GRID_ROWS,),
    ]
    vmem = pl.BlockSpec(memory_space=pltpu.VMEM)
    return pl.pallas_call(
        functools.partial(stage_kernel, cols, chunk),
        out_shape=(
            jax.ShapeDtypeStruct((slab, probes), full),
            jax.ShapeDtypeStruct((probes, probes), full),
            jax.ShapeDtypeStruct((words // GRID_ROWS, probes), half),
        ),
        in_specs=[pl.BlockSpec(memory_space=pl.ANY), vmem],
        out_specs=(vmem, vmem, vmem),
        scratch_shapes=[
            pltpu.VMEM((WINDOW, rows, chunk), half),
            pltpu.VMEM((WINDOW, chunk, probes), full),
            pltpu.VMEM((words, probes), half),
            pltpu.VMEM((words, probes), half),
            pltpu.VMEM((words, probes), half),
            pltpu.VMEM((words, probes), half),
            pltpu.VMEM((rows, probes), half),
            pltpu.VMEM((probes, rows), half),
            pltpu.VMEM((rows, probes), full),
            pltpu.VMEM((rows, probes), half),
            pltpu.VMEM((cols, slab, probes), half),
            pltpu.VMEM((cols, probes, probes), full),
            pltpu.VMEM((GRID_ROWS, probes, probes), full),
        ] + [pltpu.SemaphoreType.DMA(shape) for shape in sems],
        compiler_params=pltpu.CompilerParams(
            collective_id=0, has_side_effects=True, vmem_limit_bytes=56 * 2**20
        ),
        cost_estimate=pl.CostEstimate(
            flops=4 * rows * words * probes, bytes_accessed=2 * rows * words, transcendentals=0
        ),
    )(tile, current)


def orthonormal(product, gram_matrix, rescale):
    factor = jnp.linalg.cholesky(gram_matrix)
    solved = lax.linalg.triangular_solve(
        factor, product, left_side=False, lower=True, transpose_a=True
    )
    return (solved * rescale).astype(jnp.bfloat16)


def per_device(matrix, probes):
    tile = matrix[0]
    cols = lax.axis_size("row") // GRID_ROWS
    rescale = math.sqrt(GRID_ROWS * tile.shape[0])
    current, block = probes, None
    for _ in range(ITERS):
        image, gram_matrix, block = stage(tile, current, cols)
        current = orthonormal(image, gram_matrix, rescale)
    return (current, block[None])


def solution(mesh):
    placed = (P(("grp", "row"), None, None), P(("grp", "row"), None))
    return jax.shard_map(
        per_device,
        mesh=mesh,
        in_specs=placed,
        out_specs=(P(("grp", "row"), None), P(("grp", "row"), None, None)),
        check_vma=False,
    )
```

time: 970 us -> 324 us (0.33)
  waiting for transfers between devices: 749 us -> 0 us
  Pallas kernels: 0 us -> 266 us
  matrix products: 124 us -> 3.94 us
  other arithmetic: 66.2 us -> 47.4 us
  between operations: 14.3 us -> 0.7 us
    ppermute x12 -> x0, waiting for transfers between devices: 575 us -> none  [from_partner(): lax.ppermute(shard, axis, [(i, i ^ 1 << bit) for i in range(lax.axis_size...]
    pallas_call x0 -> x2, Pallas kernels: none -> 266 us  [stage(): pl.pallas_call(functools.partial(stage_kernel, cols, chunk), out_shape=(j...]
    psum x2 -> x0, waiting for transfers between devices: 175 us -> none  [per_device(): gram_matrix = lax.psum(local_gram, 'row')]
    dot_general x6 -> x0, matrix products: 123 us -> none  [the longest x2 63.5 us: per_device(): image = jnp.dot(tile_block, sketch, preferred_element_type=jnp.float32)]
    convert_element_type x7 -> x0, other arithmetic: 18.5 us -> none  [the longest x2 10.1 us: per_device(): partial_value.astype(jnp.bfloat16)]
  transfers between devices with their start and end apart: 14 -> 0, of which waited for: 14 -> 0; matrix products, arithmetic and copies ran while one was open for 0% -> 0% of each run, Pallas kernels for 0% -> 0%
where the time goes in v1:
time: 324 us; the launch traced here: 322 us
  Pallas kernels  266 us (82%)
  other arithmetic  47.4 us (15%)
  local copies, waits for them, and re-layouts  4.12 us (1%)
  matrix products  3.94 us (1%)
    pallas_call x2, Pallas kernels, stage(): pl.pallas_call(functools.partial(stage_kernel, cols, chunk), out_shape=(j...  266 us
    another operation x6, other arithmetic, orthonormal(): factor = jnp.linalg.cholesky(gram_matrix)  24.8 us
    another operation x4, other arithmetic, orthonormal(): lax.linalg.triangular_solve(factor, product, left_side=False, lower=True,...  20.9 us

profile of v1, /device:TPU:8, one launch (start us, length us, event | category | flops | bytes accessed | tf_op | source)
XLA Modules:
  0.0 322.3 jit_solution(13804295500215473636)
XLA Ops:
  0.6 132.5 %shard_map.41 = (f32[512,128]{1,0:T(8,128)}, f32[128,128]{1,0:T(8,128)}, bf16[4096,128]{1,0:T(8,128)(2,1)}) custom-call(bf16[2048,16384]{1,0:T(8,128)(2,1)} %bitcast.a_ref, bf16[512,128]{1,0:T(8,128)(2,1)} %cur_ref.1), custom_call_target="tpu_custom_call" | custom-call | flops 17179869184 | bytes 67108864 | tf_op jit(solution)/shard_map/pallas_call | solution.py:234
  133.1 0.9 copy.4
  134.0 0.9 fusion.9
  134.9 11.7 %cholesky.44 = f32[128,128]{1,0:T(8,128)S(1)} custom-call(f32[128,128]{1,0:T(8,128)S(1)} %fusion.9), custom_call_target="Cholesky" | custom-call | tf_op jit(solution)/shard_map/jit(cholesky)/cholesky | solution.py:268
  146.6 0.6 compare_reduce_fusion.1
  147.3 0.7 fusion.4
  147.9 9.8 %custom-call.6 = f32[1,128,128]{1,2,0:T(8,128)S(1)} custom-call(f32[1,128,128]{2,1,0:T(8,128)S(1)} %fusion.4), custom_call_target="InvertDiagBlocksLowerTriangular" | custom-call | tf_op jit(solution)/shard_map/triangular_solve/custom-call.0 | solution.py:269
  157.8 2.0 fusion.2.cur_ref
  159.7 133.7 %shard_map.42 = (f32[512,128]{1,0:T(8,128)}, f32[128,128]{1,0:T(8,128)}, bf16[4096,128]{1,0:T(8,128)(2,1)}) custom-call(bf16[2048,16384]{1,0:T(8,128)(2,1)} %bitcast.a_ref, bf16[512,128]{1,0:T(8,128)(2,1)} %fusion.2.cur_ref), custom_call_target="tpu_custom_call" | custom-call | flops 17179869184 | bytes 67108864 | tf_op jit(solution)/shard_map/pallas_call | solution.py:234
  293.4 0.9 copy.6
  294.3 0.9 fusion.7
  295.2 11.7 %cholesky.55 = f32[128,128]{1,0:T(8,128)S(1)} custom-call(f32[128,128]{1,0:T(8,128)S(1)} %fusion.7), custom_call_target="Cholesky" | custom-call | tf_op jit(solution)/shard_map/jit(cholesky)/cholesky | solution.py:268
  306.9 0.6 compare_reduce_fusion
  307.6 0.7 fusion.5
  308.2 9.8 %custom-call.7 = f32[1,128,128]{1,2,0:T(8,128)S(1)} custom-call(f32[1,128,128]{2,1,0:T(8,128)S(1)} %fusion.5), custom_call_target="InvertDiagBlocksLowerTriangular" | custom-call | tf_op jit(solution)/shard_map/triangular_solve/custom-call.0 | solution.py:269
  318.0 2.0 fusion.3
  320.0 2.3 copy.11
  (2 shorter events, 0.1 us)
